TPU v7x, 512 devices: a whole 4x4x16 slice. The times are simulated.
512 devices in a mesh: row: 32 (over y, x, core), col: 16 (over z).
Axes of the slice: x: 4, y: 4, z: 16, core: 2. Of those that a mesh axis runs over, the one named last changes fastest.
Arguments:
- matrix: float32 [12288, 12288], P('row', 'col'), may hold values from -10 to 10, as said below
- panel: float32 [12288, 64], P('row'), may hold values from -1.12763724 to 1.12763724
Outputs:
- updated: float32 [12288, 12288], P('row', 'col')
- band_block: float32 [64, 64], replicated
Inputs may be any that keep to these rules, and one draw needn't show every extreme that they name: matrix is exactly symmetric.
All inputs are finite; a program needn't handle non-finite values.
Results may differ from a plain program's by a relative error of at most 0.0002.
Values sent between devices are 32-bit elements; how exact they have to be, the bound alone decides.
A program may use at most 64 MiB of HBM per device.

v0:
```python
import jax
import jax.numpy as jnp
from jax import lax
from jax.sharding import PartitionSpec as P

precise = lax.Precision.HIGHEST


def partner_2(block, axis, stride):
    count = lax.axis_size(axis)
    route = []
    for low in range(count):
        high = low | 1 << stride
        if high != low and high < count:
            route += [(low, high), (high, low)]
    return lax.ppermute(block, axis, route)


def from_root(value, axis, source):
    kept = jnp.where(lax.axis_index(axis) == source, value, 0).astype(value.dtype)
    return lax.psum(kept, axis)


def upper_cholesky(gram_block):
    order_now = gram_block.shape[0]
    positions = jnp.arange(order_now)

    def one_column(column_index, lower_part):
        gram_column = lax.dynamic_slice_in_dim(gram_block, column_index, 1, 1)[:, 0]
        lower_row = lax.dynamic_slice_in_dim(lower_part, column_index, 1, 0)[0]
        earlier = jnp.where(positions < column_index, lower_row, 0.0)
        reduced = gram_column - jnp.dot(lower_part, earlier, precision=precise)
        pivot_value = jnp.sum(jnp.where(positions == column_index, reduced, 0.0))
        diagonal_value = jnp.sqrt(pivot_value)
        new_column = jnp.where(positions > column_index, reduced / diagonal_value, 0.0) + jnp.where(
            positions == column_index, diagonal_value, 0.0
        )
        return jnp.where(positions[None, :] == column_index, new_column[:, None], lower_part)

    lower_part = lax.fori_loop(
        0, order_now, one_column, jnp.zeros((order_now, order_now), jnp.float32)
    )
    return lower_part.T


def upper_inverse(upper_block):
    order_now = upper_block.shape[0]
    positions = jnp.arange(order_now)

    def one_row(step_count, inverse_part):
        row_at = order_now - 1 - step_count
        upper_row = lax.dynamic_slice_in_dim(upper_block, row_at, 1, 0)[0]
        diagonal_value = jnp.sum(jnp.where(positions == row_at, upper_row, 0.0))
        beyond = jnp.where(positions > row_at, upper_row, 0.0)
        unit_row = jnp.where(positions == row_at, 1.0, 0.0)
        new_row = (unit_row - jnp.dot(beyond, inverse_part, precision=precise)) / diagonal_value
        return jnp.where(positions[:, None] == row_at, new_row[None, :], inverse_part)

    return lax.fori_loop(0, order_now, one_row, jnp.zeros((order_now, order_now), jnp.float32))


def small_factor(block_in):
    order_now = block_in.shape[0]
    positions = jnp.arange(order_now)

    def one_pivot(pivot_index, state_pair):
        working, lower_whole = state_pair
        pivot_column = lax.dynamic_slice_in_dim(working, pivot_index, 1, 1)[:, 0]
        pivot_row = lax.dynamic_slice_in_dim(working, pivot_index, 1, 0)[0]
        pivot_value = jnp.sum(jnp.where(positions == pivot_index, pivot_column, 0.0))
        multipliers = jnp.where(positions > pivot_index, pivot_column / pivot_value, 0.0)
        lower_whole = lower_whole + multipliers[:, None] * (
            positions[None, :] == pivot_index
        ).astype(jnp.float32)
        working = working - multipliers[:, None] * pivot_row[None, :]
        return (working, lower_whole)

    working, lower_whole = lax.fori_loop(
        0, order_now, one_pivot, (block_in, jnp.eye(order_now, dtype=jnp.float32))
    )
    return (lower_whole, jnp.triu(working))


def body(matrix, panel):
    local_rows, local_columns = matrix.shape
    panel_width = panel.shape[1]
    row_index = lax.axis_index("row")
    current_column_index = lax.axis_index("col")
    local_inner = jnp.dot(panel.T, panel, precision=precise)
    head_rows = panel[:panel_width]
    band_factor = -upper_cholesky(local_inner)
    levels = lax.axis_size("row").bit_length() - 1
    for bit_level in range(levels):
        partner = partner_2(band_factor, "row", bit_level)
        keeps_first = row_index >> bit_level & 1 == 0
        earlier_one = jnp.where(keeps_first, band_factor, partner)
        later_one = jnp.where(keeps_first, partner, band_factor)
        paired = jnp.dot(earlier_one.T, earlier_one, precision=precise) + jnp.dot(
            later_one.T, later_one, precision=precise
        )
        band_factor = -upper_cholesky(paired)
    head_rows = from_root(head_rows, "row", 0)
    factor_inverse = upper_inverse(band_factor)
    orthogonal_rows = jnp.dot(panel, factor_inverse, precision=precise)
    orthogonal_head = jnp.dot(head_rows, factor_inverse, precision=precise)
    identity = jnp.eye(panel_width, dtype=jnp.float32)
    lower_whole, upper_whole = small_factor(orthogonal_head - identity)
    global_rows = row_index * local_rows + jnp.arange(local_rows)
    unit_rows = (global_rows[:, None] == jnp.arange(panel_width)[None, :]).astype(jnp.float32)
    reflect_rows = jnp.dot(
        orthogonal_rows - unit_rows, upper_inverse(upper_whole), precision=precise
    )
    triangle = -jnp.dot(upper_whole, upper_inverse(lower_whole.T), precision=precise)
    gathered_reflect = lax.all_gather(reflect_rows, "row", axis=0, tiled=True)
    reflect_columns = lax.dynamic_slice_in_dim(
        gathered_reflect, current_column_index * local_columns, local_columns, 0
    )
    partial_product = lax.dot_general(
        matrix, reflect_rows, (((0,), (0,)), ((), ())), precision=precise
    )
    product = lax.psum(partial_product, "row")
    applied_cols = jnp.dot(product, triangle, precision=precise)
    inner_part = jnp.dot(reflect_columns.T, applied_cols, precision=precise)
    inner_total = lax.psum(inner_part, "col")
    coupling = jnp.dot(triangle.T, inner_total, precision=precise)
    corrected_cols = applied_cols - 0.5 * jnp.dot(reflect_columns, coupling, precision=precise)
    gathered_corrected = lax.all_gather(corrected_cols, "col", axis=0, tiled=True)
    corrected_rows = lax.dynamic_slice_in_dim(
        gathered_corrected, row_index * local_rows, local_rows, 0
    )
    left_factor = jnp.concatenate([reflect_rows, corrected_rows], 1)
    right_factor = jnp.concatenate([corrected_cols, reflect_columns], 1)
    updated = matrix - lax.dot_general(
        left_factor, right_factor, (((1,), (1,)), ((), ())), precision=precise
    )
    return (updated, band_factor)


def solution(mesh):
    return jax.shard_map(
        body,
        mesh=mesh,
        in_specs=(P("row", "col"), P("row", None)),
        out_specs=(P("row", "col"), P()),
        check_vma=False,
    )
```

profile of v0, /device:TPU:14, one launch (start us, length us, event | category | flops | bytes accessed | tf_op | source)
XLA Modules:
  0.0 1399.8 jit_solution(851780001571916975)
XLA Ops:
  7.2 1.2 fusion.154
  8.5 101.3 %while.159 = (s32[]{:T(128)}, f32[64,64]{1,0:T(8,128)S(1)}, f32[64,64]{0,1:T(8,128)S(1)}, s32[]{:T(128)}, s32[]{:T(128)}) while((s32[]{:T(128)}, f32[64,64]{1,0:T(8,128)S(1)}, f32[64,64]{0,1:T(8,128)S(1)}, s32[]{:T(128)}, s32[]{:T(128)}) %tuple.367), condition=%wide.region_2.3_spmd.clone.clone, body=%wide.region_0.2_spmd.clone.clone.sunk | while | flops 62274 | bytes 102632 | solution.py:40
  109.8 1.9 collective-permute-start
  111.9 1.1 collective-permute-done
  113.4 101.3 %while.160 = (s32[]{:T(128)}, f32[64,64]{1,0:T(8,128)S(1)}, f32[64,64]{0,1:T(8,128)S(1)}, s32[]{:T(128)}, s32[]{:T(128)}) while((s32[]{:T(128)}, f32[64,64]{1,0:T(8,128)S(1)}, f32[64,64]{0,1:T(8,128)S(1)}, s32[]{:T(128)}, s32[]{:T(128)}) %tuple.370), condition=%wide.region_5.6_spmd.clone.clone, body=%wide.region_3.5_spmd.clone.clone.sunk | while | flops 62274 | bytes 102632 | solution.py:40
  214.7 2.7 collective-permute-start.1
  217.5 3.0 collective-permute-done.1
  220.9 101.3 %while.161 = (s32[]{:T(128)}, f32[64,64]{1,0:T(8,128)S(1)}, f32[64,64]{0,1:T(8,128)S(1)}, s32[]{:T(128)}, s32[]{:T(128)}) while((s32[]{:T(128)}, f32[64,64]{1,0:T(8,128)S(1)}, f32[64,64]{0,1:T(8,128)S(1)}, s32[]{:T(128)}, s32[]{:T(128)}) %tuple.373), condition=%wide.region_8.9_spmd.clone.clone, body=%wide.region_6.8_spmd.clone.clone.sunk | while | flops 62274 | bytes 102632 | solution.py:40
  322.3 3.3 collective-permute-start.2
  325.6 4.0 collective-permute-done.2
  330.1 101.3 %while.162 = (s32[]{:T(128)}, f32[64,64]{1,0:T(8,128)S(1)}, f32[64,64]{0,1:T(8,128)S(1)}, s32[]{:T(128)}, s32[]{:T(128)}) while((s32[]{:T(128)}, f32[64,64]{1,0:T(8,128)S(1)}, f32[64,64]{0,1:T(8,128)S(1)}, s32[]{:T(128)}, s32[]{:T(128)}) %tuple.376), condition=%wide.region_11.12_spmd.clone.clone, body=%wide.region_9.11_spmd.clone.clone.sunk | while | flops 62274 | bytes 102632 | solution.py:40
  431.4 4.1 collective-permute-start.3
  435.5 1.8 collective-permute-done.3
  437.9 101.3 %while.163 = (s32[]{:T(128)}, f32[64,64]{1,0:T(8,128)S(1)}, f32[64,64]{0,1:T(8,128)S(1)}, s32[]{:T(128)}, s32[]{:T(128)}) while((s32[]{:T(128)}, f32[64,64]{1,0:T(8,128)S(1)}, f32[64,64]{0,1:T(8,128)S(1)}, s32[]{:T(128)}, s32[]{:T(128)}) %tuple.379), condition=%wide.region_14.15_spmd.clone.clone, body=%wide.region_12.14_spmd.clone.clone.sunk | while | flops 62274 | bytes 102632 | solution.py:40
  539.2 4.0 collective-permute-start.4
  543.3 102.9 %psum.21 = f32[64,64]{1,0:T(8,128)S(1)} all-reduce(f32[64,64]{1,0:T(8,128)S(1)} %broadcast_select_fusion.12), channel_id=1, replica_groups=mesh['row'=32,'col'=16] {'row'}, use_global_device_ids=true, to_apply=%region_21.22 | all-reduce | flops 4096 | bytes 32768 | tf_op jit(solution)/shard_map/psum | solution.py:21
  646.6 102.2 %while.164 = (s32[]{:T(128)}, f32[64,64]{1,0:T(8,128)S(1)}, f32[64,64]{0,1:T(8,128)S(1)}, s32[]{:T(128)}, s32[]{:T(128)}) while((s32[]{:T(128)}, f32[64,64]{1,0:T(8,128)S(1)}, f32[64,64]{0,1:T(8,128)S(1)}, s32[]{:T(128)}, s32[]{:T(128)}) %tuple.382), condition=%wide.region_17.18_spmd.clone.clone, body=%wide.region_15.17_spmd.clone.clone.sunk | while | flops 62274 | bytes 102632 | solution.py:40
  749.0 95.1 %while.165 = (s32[]{:T(128)}, f32[64,64]{1,0:T(8,128)S(1)}, f32[64,64]{1,0:T(8,128)S(1)}, s32[]{:T(128)}, s32[]{:T(128)}, /*index=5*/s32[]{:T(128)}, s32[]{:T(128)}) while((s32[]{:T(128)}, f32[64,64]{1,0:T(8,128)S(1)}, f32[64,64]{1,0:T(8,128)S(1)}, s32[]{:T(128)}, s32[]{:T(128)}, /*index=5*/s32[]{:T(128)}, ...), condition=%wide.region_20.21_spmd.clone.clone, body=%wide.region_18.20_spmd.clone.clone.sunk | while | flops 62086 | bytes 69153 | solution.py:59
  844.3 100.7 %while.158 = (s32[]{:T(128)}, f32[64,64]{0,1:T(8,128)S(1)}, f32[64,64]{0,1:T(8,128)S(1)}, s32[]{:T(128)}) while((s32[]{:T(128)}, f32[64,64]{0,1:T(8,128)S(1)}, f32[64,64]{0,1:T(8,128)S(1)}, s32[]{:T(128)}) %tuple.388), condition=%wide.region_24.25_spmd.clone.clone, body=%wide.region_22.24_spmd.clone.clone.sunk | while | flops 16897 | bytes 69965 | solution.py:78
  945.1 95.1 %while.166 = (s32[]{:T(128)}, f32[64,64]{1,0:T(8,128)S(1)}, f32[64,64]{1,0:T(8,128)S(1)}, s32[]{:T(128)}, s32[]{:T(128)}, /*index=5*/s32[]{:T(128)}, s32[]{:T(128)}) while((s32[]{:T(128)}, f32[64,64]{1,0:T(8,128)S(1)}, f32[64,64]{1,0:T(8,128)S(1)}, s32[]{:T(128)}, s32[]{:T(128)}, /*index=5*/s32[]{:T(128)}, ...), condition=%wide.region_27.28_spmd.clone.clone, body=%wide.region_25.27_spmd.clone.clone.sunk | while | flops 62086 | bytes 69153 | solution.py:59
  1040.8 1.5 convolution_bitcast_fusion.9
  1043.2 103.2 %while.167 = (s32[]{:T(128)}, f32[64,64]{1,0:T(8,128)S(1)}, f32[64,64]{1,0:T(8,128)S(1)}, s32[]{:T(128)}, s32[]{:T(128)}, /*index=5*/s32[]{:T(128)}, s32[]{:T(128)}) while((s32[]{:T(128)}, f32[64,64]{1,0:T(8,128)S(1)}, f32[64,64]{1,0:T(8,128)S(1)}, s32[]{:T(128)}, s32[]{:T(128)}, /*index=5*/s32[]{:T(128)}, ...), condition=%wide.region_31.32_spmd.clone.clone, body=%wide.region_29.31_spmd.clone.clone.sunk | while | flops 62086 | bytes 69153 | solution.py:59
  1058.4 0.8 fusion.236
  1060.0 0.8 fusion.236
  1061.6 0.8 fusion.236
  1063.2 0.8 fusion.236
  1064.8 0.8 fusion.236
  1066.4 0.8 fusion.236
  1068.1 0.8 fusion.236
  1082.6 0.8 fusion.236
  1098.7 0.8 fusion.236
  1100.3 0.8 fusion.236
  1101.9 0.8 fusion.236
  1103.5 0.8 fusion.236
  1105.1 0.8 fusion.236
  1106.7 0.8 fusion.236
  1116.4 0.8 fusion.236
  1119.6 0.8 fusion.236
  1143.8 0.8 fusion.236
  1146.5 45.9 %all-reduce.2.cloned.1.call-done = f32[768,64]{0,1:T(8,128)} async-done(((f32[768,64]{0,1:T(8,128)}), f32[768,64]{0,1:T(8,128)}) %all-reduce.2.cloned.1.call-update) | async-done | bytes 196624 | tf_op jit(solution)/shard_map/psum | solution.py:121
  1192.4 1.3 fusion.156
  1193.7 62.0 %all-gather.3.cloned.1.call-done = f32[12288,64]{0,1:T(8,128)} async-done(((f32[384,64]{0,1:T(8,128)}), f32[12288,64]{0,1:T(8,128)}) %all-gather.3.cloned.1.call-update) | async-done | bytes 3145744 | tf_op jit(solution)/shard_map/all_gather | solution.py:114
  1255.6 0.9 constant_dynamic-slice_fusion.8
  1256.9 56.9 %psum.23 = f32[64,64]{1,0:T(8,128)S(1)} all-reduce(f32[64,64]{1,0:T(8,128)S(1)} %fusion.157), channel_id=1, replica_groups=mesh['row'=32,'col'=16] {'col'}, use_global_device_ids=true, to_apply=%region_32.33 | all-reduce | flops 4096 | bytes 32768 | tf_op jit(solution)/shard_map/psum | solution.py:124
  1314.0 1.0 fusion.118
  1315.1 74.2 %all-gather.5.cloned.1.call-done = f32[12288,64]{0,1:T(8,128)} async-done(((f32[768,64]{0,1:T(8,128)}), f32[12288,64]{0,1:T(8,128)}) %all-gather.5.cloned.1.call-update) | async-done | bytes 3145744 | tf_op jit(solution)/shard_map/all_gather | solution.py:127
  1389.3 0.9 constant_dynamic-slice_fusion.7
  1390.2 3.1 convolution_subtract_fusion
  (3056 shorter events, 716.6 us)
Async XLA Ops:
  7.2 104.6 %slice-start = ((f32[384,64]{0,1:T(8,128)}), f32[64,64]{0,1:T(8,128)S(1)}, s32[]{:S(2)}) async-start(f32[384,64]{0,1:T(8,128)} %param.23), calls=%async_computation.3 | async-start | bytes 65536 | tf_op jit(solution)/shard_map/slice | solution.py:90
  7.2 1185.2 %all-reduce.2.cloned.1.call-start = ((), (), s32[]{:S(2)}) async-start(), calls=%async_computation | async-start | bytes 393216 | tf_op jit(solution)/shard_map/psum | solution.py:121
  109.8 3.1 collective-permute-start
  214.7 5.8 collective-permute-start.1
  322.3 7.3 collective-permute-start.2
  431.4 6.0 collective-permute-start.3
  539.2 107.0 %collective-permute-start.4 = (f32[64,64]{0,1:T(8,128)S(1)}, f32[64,64]{0,1:T(8,128)S(1)}, u32[]{:S(2)}, u32[]{:S(2)}) collective-permute-start(f32[64,64]{0,1:T(8,128)S(1)} %negate_bitcast_fusion.1), channel_id=1, source_target_pairs={{0,256},{256,0},{16,272},{272,16},{32,288},{288,32},{48,304},{304,... | collective-permute-start | bytes 49160 | tf_op jit(solution)/shard_map/ppermute | solution.py:16
  748.9 291.3 %copy-start.3 = (f32[384,64]{0,1:T(8,128)S(1)}, f32[384,64]{0,1:T(8,128)}, u32[]{:S(2)}) copy-start(f32[384,64]{0,1:T(8,128)} %param.23) | copy-start | bytes 294916
  749.0 291.9 %copy-start = (f32[384,768]{1,0:T(8,128)S(1)}, f32[384,768]{1,0:T(8,128)}, u32[]{:S(2)}) copy-start(f32[384,768]{1,0:T(8,128)} %param.22) | copy-start | bytes 3538948
  844.1 196.8 %copy-start.4 = (f32[64,64]{1,0:T(8,128)}, f32[64,64]{1,0:T(8,128)S(1)}, u32[]{:S(2)}) copy-start(f32[64,64]{1,0:T(8,128)S(1)} %get-tuple-element.1720) | copy-start | bytes 49156
  1040.8 1.6 copy-start.1
  1042.4 213.3 %all-gather.3.cloned.1.call-start = ((), (), s32[]{:S(2)}) async-start(), calls=%async_computation.1 | async-start | bytes 3244032 | tf_op jit(solution)/shard_map/all_gather | solution.py:114
  1043.1 346.2 %all-gather.5.cloned.1.call-start = ((), (), s32[]{:S(2)}) async-start(), calls=%async_computation.2 | async-start | bytes 3342336 | tf_op jit(solution)/shard_map/all_gather | solution.py:127
  1146.5 243.7 %copy-start.2 = (f32[384,64]{0,1:T(8,128)S(1)}, f32[384,64]{0,1:T(8,128)}, u32[]{:S(2)}) copy-start(f32[384,64]{0,1:T(8,128)} %copy-done.1) | copy-start | bytes 294916
Sparse Core Ops, SparseCore 0:
  1042.5 149.8 all-reduce.1
  1196.1 59.4 all-gather.2
  1315.2 74.0 all-gather.4
where the time goes:
time: 1410 us; the launch traced here: 1400 us
  matrix products  464 us (33%)
  loops' own time  277 us (20%)
  other arithmetic  262 us (19%)
  waiting for transfers between devices  193 us (14%)
  blocking collectives  160 us (11%)
  starting transfers between devices  16.2 us (1%)
  between operations  14.2 us (1%)
    dot_general x384, matrix products, one_column(): reduced = gram_column - jnp.dot(lower_part, earlier, precision=precise)  299 us
    another operation x6, loops' own time, upper_cholesky(): lax.fori_loop(0, order_now, one_column, jnp.zeros((order_now, order_now),...  274 us
    dot_general x192, matrix products, one_row(): jnp.dot(beyond, inverse_part, precision=precise)  154 us
    reduce_sum x192, other arithmetic, one_row(): diagonal_value = jnp.sum(jnp.where(positions == row_at, upper_row, 0.0))  123 us
    psum x1, blocking collectives, from_root(): return lax.psum(kept, axis)  103 us
    all_gather x1, waiting for transfers between devices, body(): lax.all_gather(corrected_cols, 'col', axis=0, tiled=True)  74.2 us
    all_gather x1, waiting for transfers between devices, body(): gathered_reflect = lax.all_gather(reflect_rows, 'row', axis=0, tiled=True)  62 us
    psum x1, blocking collectives, body(): inner_total = lax.psum(inner_part, 'col')  56.9 us
  transfers between devices with their start and end apart: 8, of which 7 were waited for; matrix products, arithmetic and copies ran while one was open for 7% of the time, Pallas kernels for 0%

commit v1 on v0

--- a/solution.py
+++ b/solution.py
@@ -124,7 +124,9 @@
     inner_total = lax.psum(inner_part, "col")
     coupling = jnp.dot(triangle.T, inner_total, precision=precise)
     corrected_cols = applied_cols - 0.5 * jnp.dot(reflect_columns, coupling, precision=precise)
-    gathered_corrected = lax.all_gather(corrected_cols, "col", axis=0, tiled=True)
+    gathered_corrected = jnp.concatenate(
+        lax.all_to_all(jnp.stack([corrected_cols] * lax.axis_size("col")), "col", 0, 0), axis=0
+    )
     corrected_rows = lax.dynamic_slice_in_dim(
         gathered_corrected, row_index * local_rows, local_rows, 0
     )

time: 1410 us -> 1470 us (1.043)
  the two profiles are of different devices: /device:TPU:14 before, /device:TPU:32 now
where the time goes in v1:
time: 1470 us; the launch traced here: 1460 us
  matrix products  462 us (31%)
  loops' own time  277 us (19%)
  other arithmetic  262 us (18%)
  waiting for transfers between devices  221 us (15%)
  blocking collectives  179 us (12%)
  starting transfers between devices  29.3 us (2%)
  local copies, waits for them, and re-layouts  16.8 us (1%)
    dot_general x384, matrix products, one_column(): reduced = gram_column - jnp.dot(lower_part, earlier, precision=precise)  299 us
    another operation x6, loops' own time, upper_cholesky(): lax.fori_loop(0, order_now, one_column, jnp.zeros((order_now, order_now),...  274 us
    dot_general x192, matrix products, one_row(): jnp.dot(beyond, inverse_part, precision=precise)  154 us
    all_to_all x1, waiting for transfers between devices, body(): lax.all_to_all(jnp.stack([corrected_cols] * lax.axis_size('col')), 'col',...  125 us
    psum x1, blocking collectives, from_root(): return lax.psum(kept, axis)  124 us
    reduce_sum x192, other arithmetic, one_row(): diagonal_value = jnp.sum(jnp.where(positions == row_at, upper_row, 0.0))  123 us
    all_gather x1, waiting for transfers between devices, body(): gathered_reflect = lax.all_gather(reflect_rows, 'row', axis=0, tiled=True)  62.1 us
    psum x1, blocking collectives, body(): inner_total = lax.psum(inner_part, 'col')  55.5 us
  transfers between devices with their start and end apart: 8, of which 7 were waited for; matrix products, arithmetic and copies ran while one was open for 7% of the time, Pallas kernels for 0%

profile of v1, /device:TPU:32, one launch (start us, length us, event | category | flops | bytes accessed | tf_op | source)
XLA Modules:
  0.0 1462.9 jit_solution(9975379302553752711)
XLA Ops:
  7.2 1.2 fusion.154
  8.5 101.3 %while.159 = (s32[]{:T(128)}, f32[64,64]{1,0:T(8,128)S(1)}, f32[64,64]{0,1:T(8,128)S(1)}, s32[]{:T(128)}, s32[]{:T(128)}) while((s32[]{:T(128)}, f32[64,64]{1,0:T(8,128)S(1)}, f32[64,64]{0,1:T(8,128)S(1)}, s32[]{:T(128)}, s32[]{:T(128)}) %tuple.374), condition=%wide.region_2.3_spmd.clone.clone, body=%wide.region_0.2_spmd.clone.clone.sunk | while | flops 62274 | bytes 102632 | solution.py:40
  109.8 1.9 collective-permute-start
  111.9 1.1 collective-permute-done
  113.4 101.3 %while.160 = (s32[]{:T(128)}, f32[64,64]{1,0:T(8,128)S(1)}, f32[64,64]{0,1:T(8,128)S(1)}, s32[]{:T(128)}, s32[]{:T(128)}) while((s32[]{:T(128)}, f32[64,64]{1,0:T(8,128)S(1)}, f32[64,64]{0,1:T(8,128)S(1)}, s32[]{:T(128)}, s32[]{:T(128)}) %tuple.377), condition=%wide.region_5.6_spmd.clone.clone, body=%wide.region_3.5_spmd.clone.clone.sunk | while | flops 62274 | bytes 102632 | solution.py:40
  214.7 3.4 collective-permute-start.1
  218.1 2.4 collective-permute-done.1
  221.0 101.3 %while.161 = (s32[]{:T(128)}, f32[64,64]{1,0:T(8,128)S(1)}, f32[64,64]{0,1:T(8,128)S(1)}, s32[]{:T(128)}, s32[]{:T(128)}) while((s32[]{:T(128)}, f32[64,64]{1,0:T(8,128)S(1)}, f32[64,64]{0,1:T(8,128)S(1)}, s32[]{:T(128)}, s32[]{:T(128)}) %tuple.380), condition=%wide.region_8.9_spmd.clone.clone, body=%wide.region_6.8_spmd.clone.clone.sunk | while | flops 62274 | bytes 102632 | solution.py:40
  322.3 4.9 collective-permute-start.2
  327.3 2.3 collective-permute-done.2
  330.1 101.3 %while.162 = (s32[]{:T(128)}, f32[64,64]{1,0:T(8,128)S(1)}, f32[64,64]{0,1:T(8,128)S(1)}, s32[]{:T(128)}, s32[]{:T(128)}) while((s32[]{:T(128)}, f32[64,64]{1,0:T(8,128)S(1)}, f32[64,64]{0,1:T(8,128)S(1)}, s32[]{:T(128)}, s32[]{:T(128)}) %tuple.383), condition=%wide.region_11.12_spmd.clone.clone, body=%wide.region_9.11_spmd.clone.clone.sunk | while | flops 62274 | bytes 102632 | solution.py:40
  431.4 3.5 collective-permute-start.3
  434.9 2.3 collective-permute-done.3
  437.6 101.3 %while.163 = (s32[]{:T(128)}, f32[64,64]{1,0:T(8,128)S(1)}, f32[64,64]{0,1:T(8,128)S(1)}, s32[]{:T(128)}, s32[]{:T(128)}) while((s32[]{:T(128)}, f32[64,64]{1,0:T(8,128)S(1)}, f32[64,64]{0,1:T(8,128)S(1)}, s32[]{:T(128)}, s32[]{:T(128)}) %tuple.386), condition=%wide.region_14.15_spmd.clone.clone, body=%wide.region_12.14_spmd.clone.clone.sunk | while | flops 62274 | bytes 102632 | solution.py:40
  539.0 5.1 collective-permute-start.4
  544.2 123.8 %psum.21 = f32[64,64]{1,0:T(8,128)S(1)} all-reduce(f32[64,64]{1,0:T(8,128)S(1)} %broadcast_select_fusion.12), channel_id=1, replica_groups=mesh['row'=32,'col'=16] {'row'}, use_global_device_ids=true, to_apply=%region_21.22 | all-reduce | flops 4096 | bytes 32768 | tf_op jit(solution)/shard_map/psum | solution.py:21
  668.4 102.2 %while.164 = (s32[]{:T(128)}, f32[64,64]{1,0:T(8,128)S(1)}, f32[64,64]{0,1:T(8,128)S(1)}, s32[]{:T(128)}, s32[]{:T(128)}) while((s32[]{:T(128)}, f32[64,64]{1,0:T(8,128)S(1)}, f32[64,64]{0,1:T(8,128)S(1)}, s32[]{:T(128)}, s32[]{:T(128)}) %tuple.389), condition=%wide.region_17.18_spmd.clone.clone, body=%wide.region_15.17_spmd.clone.clone.sunk | while | flops 62274 | bytes 102632 | solution.py:40
  770.8 95.1 %while.165 = (s32[]{:T(128)}, f32[64,64]{1,0:T(8,128)S(1)}, f32[64,64]{1,0:T(8,128)S(1)}, s32[]{:T(128)}, s32[]{:T(128)}, /*index=5*/s32[]{:T(128)}, s32[]{:T(128)}) while((s32[]{:T(128)}, f32[64,64]{1,0:T(8,128)S(1)}, f32[64,64]{1,0:T(8,128)S(1)}, s32[]{:T(128)}, s32[]{:T(128)}, /*index=5*/s32[]{:T(128)}, ...), condition=%wide.region_20.21_spmd.clone.clone, body=%wide.region_18.20_spmd.clone.clone.sunk | while | flops 62086 | bytes 69153 | solution.py:59
  866.7 100.7 %while.158 = (s32[]{:T(128)}, f32[64,64]{0,1:T(8,128)S(1)}, f32[64,64]{0,1:T(8,128)S(1)}, s32[]{:T(128)}) while((s32[]{:T(128)}, f32[64,64]{0,1:T(8,128)S(1)}, f32[64,64]{0,1:T(8,128)S(1)}, s32[]{:T(128)}) %tuple.395), condition=%wide.region_24.25_spmd.clone.clone, body=%wide.region_22.24_spmd.clone.clone.sunk | while | flops 16897 | bytes 69965 | solution.py:78
  967.6 95.1 %while.166 = (s32[]{:T(128)}, f32[64,64]{1,0:T(8,128)S(1)}, f32[64,64]{1,0:T(8,128)S(1)}, s32[]{:T(128)}, s32[]{:T(128)}, /*index=5*/s32[]{:T(128)}, s32[]{:T(128)}) while((s32[]{:T(128)}, f32[64,64]{1,0:T(8,128)S(1)}, f32[64,64]{1,0:T(8,128)S(1)}, s32[]{:T(128)}, s32[]{:T(128)}, /*index=5*/s32[]{:T(128)}, ...), condition=%wide.region_27.28_spmd.clone.clone, body=%wide.region_25.27_spmd.clone.clone.sunk | while | flops 62086 | bytes 69153 | solution.py:59
  1063.3 1.5 convolution_bitcast_fusion.9
  1065.5 103.2 %while.167 = (s32[]{:T(128)}, f32[64,64]{1,0:T(8,128)S(1)}, f32[64,64]{1,0:T(8,128)S(1)}, s32[]{:T(128)}, s32[]{:T(128)}, /*index=5*/s32[]{:T(128)}, s32[]{:T(128)}) while((s32[]{:T(128)}, f32[64,64]{1,0:T(8,128)S(1)}, f32[64,64]{1,0:T(8,128)S(1)}, s32[]{:T(128)}, s32[]{:T(128)}, /*index=5*/s32[]{:T(128)}, ...), condition=%wide.region_31.32_spmd.clone.clone, body=%wide.region_29.31_spmd.clone.clone.sunk | while | flops 62086 | bytes 69153 | solution.py:59
  1066.3 0.8 fusion.236
  1067.9 0.8 fusion.236
  1069.5 0.8 fusion.236
  1087.2 0.8 fusion.236
  1098.5 0.8 fusion.236
  1109.8 0.8 fusion.236
  1111.4 0.8 fusion.236
  1113.0 0.8 fusion.236
  1114.6 0.8 fusion.236
  1116.2 0.8 fusion.236
  1117.8 0.8 fusion.236
  1119.4 0.8 fusion.236
  1140.4 0.8 fusion.236
  1142.0 0.8 fusion.236
  1143.6 0.8 fusion.236
  1150.1 0.8 fusion.236
  1168.9 25.8 %all-reduce.2.cloned.1.call-done = f32[768,64]{0,1:T(8,128)} async-done(((f32[768,64]{0,1:T(8,128)}), f32[768,64]{0,1:T(8,128)}) %all-reduce.2.cloned.1.call-update) | async-done | bytes 196624 | tf_op jit(solution)/shard_map/psum | solution.py:121
  1194.7 1.3 fusion.156
  1196.0 62.1 %all-gather.2.cloned.1.call-done = f32[12288,64]{0,1:T(8,128)} async-done(((f32[384,64]{0,1:T(8,128)}), f32[12288,64]{0,1:T(8,128)}) %all-gather.2.cloned.1.call-update) | async-done | bytes 3145744 | tf_op jit(solution)/shard_map/all_gather | solution.py:114
  1258.1 0.9 constant_dynamic-slice_fusion.8
  1259.4 55.5 %psum.23 = f32[64,64]{1,0:T(8,128)S(1)} all-reduce(f32[64,64]{1,0:T(8,128)S(1)} %fusion.157), channel_id=1, replica_groups=mesh['row'=32,'col'=16] {'col'}, use_global_device_ids=true, to_apply=%region_32.33 | all-reduce | flops 4096 | bytes 32768 | tf_op jit(solution)/shard_map/psum | solution.py:124
  1315.5 2.0 stack.2
  1317.4 10.4 all-to-all-start
  1327.9 124.7 %all-to-all-done = f32[16,768,64]{1,2,0:T(8,128)S(1)} async-done(((f32[16,768,64]{1,2,0:T(8,128)}), f32[16,768,64]{1,2,0:T(8,128)S(1)}, u32[]{:S(2)}, u32[]{:S(2)}) %all-to-all-start) | async-done | bytes 3145760 | tf_op jit(solution)/shard_map/all_to_all | solution.py:128
  1452.9 0.9 copy-done.1
  1453.8 2.2 convolution_subtract_fusion
  (3059 shorter events, 718.7 us)
Async XLA Ops:
  7.2 104.6 %slice-start = ((f32[384,64]{0,1:T(8,128)}), f32[64,64]{0,1:T(8,128)S(1)}, s32[]{:S(2)}) async-start(f32[384,64]{0,1:T(8,128)} %param.23), calls=%async_computation.3 | async-start | bytes 65536 | tf_op jit(solution)/shard_map/slice | solution.py:90
  7.2 1187.5 %all-reduce.2.cloned.1.call-start = ((), (), s32[]{:S(2)}) async-start(), calls=%async_computation.1 | async-start | bytes 393216 | tf_op jit(solution)/shard_map/psum | solution.py:121
  109.8 3.1 collective-permute-start
  214.7 5.8 collective-permute-start.1
  322.3 7.3 collective-permute-start.2
  431.4 5.8 collective-permute-start.3
  539.0 129.0 %collective-permute-start.4 = (f32[64,64]{0,1:T(8,128)S(1)}, f32[64,64]{0,1:T(8,128)S(1)}, u32[]{:S(2)}, u32[]{:S(2)}) collective-permute-start(f32[64,64]{0,1:T(8,128)S(1)} %negate_bitcast_fusion.1), channel_id=1, source_target_pairs={{0,256},{256,0},{16,272},{272,16},{32,288},{288,32},{48,304},{304,... | collective-permute-start | bytes 49160 | tf_op jit(solution)/shard_map/ppermute | solution.py:16
  770.8 291.9 %copy-start.4 = (f32[384,64]{0,1:T(8,128)S(1)}, f32[384,64]{0,1:T(8,128)}, u32[]{:S(2)}) copy-start(f32[384,64]{0,1:T(8,128)} %param.23) | copy-start | bytes 294916
  770.8 292.5 %copy-start = (f32[384,768]{1,0:T(8,128)S(1)}, f32[384,768]{1,0:T(8,128)}, u32[]{:S(2)}) copy-start(f32[384,768]{1,0:T(8,128)} %param.22) | copy-start | bytes 3538948
  865.9 0.6 copy-start.5
  1063.2 1.6 copy-start.2
  1064.8 193.3 %all-gather.2.cloned.1.call-start = ((), (), s32[]{:S(2)}) async-start(), calls=%async_computation.2 | async-start | bytes 3244032 | tf_op jit(solution)/shard_map/all_gather | solution.py:114
  1317.4 135.1 %all-to-all-start = ((f32[16,768,64]{1,2,0:T(8,128)}), f32[16,768,64]{1,2,0:T(8,128)S(1)}, u32[]{:S(2)}, u32[]{:S(2)}) async-start(f32[16,768,64]{1,2,0:T(8,128)} %stack.2), calls=%async_computation | async-start | bytes 6291456 | tf_op jit(solution)/shard_map/all_to_all | solution.py:128
  1452.5 1.3 copy-start.1
  1452.5 1.3 copy-start.3
Sparse Core Ops, SparseCore 0:
  1064.9 129.7 all-reduce.1
  1198.4 59.6 all-gather.1
